TPU v7x, 1024 devices: a whole 4x4x32 slice. The times are simulated.
1024 devices in a mesh: dp: 8 (over x, core), shard: 128 (over z, y).
Axes of the slice: x: 4, y: 4, z: 32, core: 2. Of those that a mesh axis runs over, the one named last changes fastest.
Arguments:
- gradients: float32 [8, 3, 448, 32768], P('dp', None, None, 'shard'), may hold values from -6 to 6
- momentum: float32 [3, 448, 32768], P(None, 'dp', 'shard'), may hold values from -6 to 6
Outputs:
- momentum_out: float32 [3, 448, 32768], P(None, 'dp', 'shard')
- update: bfloat16 [3, 448, 32768], P(None, 'dp', 'shard')
All inputs are finite; a program needn't handle non-finite values.
Results may differ from a plain program's by a relative error of at most 0.018.
The roundings to bfloat16 on the way count: a program that leaves them out, or rounds other values in their place, can miss the bound.
Values may be sent and summed in bfloat16 or wider, within the bound.
No kernel may reach another device: no remote copies, remote signals or barrier semaphores. Data moves between devices by JAX's collectives and lax.ppermute only.
A program may use at most 128 MiB of HBM per device.

v0:
```python
import jax
import jax.numpy as jnp
from jax import lax
from jax.sharding import PartitionSpec as P

R = 7168
C = 2048
ITERS = 5
BR = 16


COEF_A = 3.4445
COEF_B = -4.775
COEF_C = 2.0315
DECAY = 0.95
EPSILON = 1e-07
ROW_SCALE = 0.2


def newton_schulz(blocks):
    squares = jnp.sum(jnp.square(blocks.astype(jnp.float32)), axis=(1, 2))
    current = (blocks.astype(jnp.float32) / (jnp.sqrt(squares) + EPSILON)[:, None, None]).astype(
        jnp.bfloat16
    )
    for sweep_index in range(ITERS):
        gram = jnp.einsum(
            "kri,ksi->krs", current, current, preferred_element_type=jnp.float32
        ).astype(jnp.bfloat16)
        squared = jnp.einsum("krs,kst->krt", gram, gram, preferred_element_type=jnp.float32)
        polynomial = (COEF_B * gram.astype(jnp.float32) + COEF_C * squared).astype(jnp.bfloat16)
        product = jnp.einsum(
            "krs,ksi->kri", polynomial, current, preferred_element_type=jnp.float32
        )
        current = (COEF_A * current.astype(jnp.float32) + product).astype(jnp.bfloat16)
    factor = ROW_SCALE * jnp.sqrt(jnp.float32(R))
    return (current.astype(jnp.float32) * factor).astype(jnp.bfloat16)


def orthogonalize(tile_rows, first_pos):
    owners_count = lax.axis_size("shard")
    span_count, local_flat = tile_rows.shape
    base_pos = first_pos // owners_count * owners_count
    leading = first_pos - base_pos
    capacity = (first_pos + span_count - 1) // owners_count - first_pos // owners_count + 1
    trailing = capacity * owners_count - leading - span_count
    padded = jnp.pad(tile_rows, ((leading, trailing), (0, 0)))
    outgoing = padded.reshape(capacity, owners_count, local_flat)
    arrived = lax.all_to_all(outgoing, "shard", split_axis=1, concat_axis=2, tiled=True)
    results = newton_schulz(arrived.reshape(capacity, BR, C))
    returned = lax.all_to_all(
        results.reshape(capacity, 1, BR * C), "shard", split_axis=2, concat_axis=1, tiled=True
    )
    flat = returned.reshape(capacity * owners_count, local_flat)
    return flat[leading : leading + span_count]


def advance(summed, previous, first_pos):
    count_mats, local_blocks, local_flat = previous.shape
    momentum_next = DECAY * previous + summed
    nesterov = (summed + DECAY * momentum_next).astype(jnp.bfloat16)
    tile_rows = nesterov.reshape(count_mats * local_blocks, local_flat)
    finished = orthogonalize(tile_rows, first_pos)
    return (momentum_next, finished.reshape(previous.shape))


def shards(gradients, momentum):
    summed = lax.psum_scatter(gradients, "dp", scatter_dimension=2, tiled=True)[0]
    momentum_next, update = advance(summed, momentum, 0)
    return (momentum_next, update)


def solution(mesh):
    placed = (P("dp", None, None, "shard"), P(None, "dp", "shard"))
    return jax.shard_map(
        shards,
        mesh=mesh,
        in_specs=placed,
        out_specs=(P(None, "dp", "shard"), P(None, "dp", "shard")),
        check_vma=False,
    )
```

profile of v0, /device:TPU:38, one launch (start us, length us, event | category | flops | bytes accessed | tf_op | source)
XLA Modules:
  0.0 456.1 jit_solution(5409254399067729633)
XLA Ops:
  7.2 0.0 reduce-scatter.2.cloned.1.call-start
  7.2 0.7 reduce-scatter.2.cloned.1.call-update
  7.9 57.8 %reduce-scatter.2.cloned.1.call-done = f32[1,3,56,256]{3,2,1,0:T(8,128)} async-done(((f32[1,3,448,256]{3,2,1,0:T(8,128)}), f32[1,3,56,256]{3,2,1,0:T(8,128)}) %reduce-scatter.2.cloned.1.call-update) | async-done | bytes 172048 | tf_op jit(solution)/shard_map/reduce_scatter | solution.py:67
  65.7 1.7 fusion.18
  67.4 0.1 copy.10
  67.5 57.9 %all_to_all.8 = bf16[2,128,256]{2,0,1:T(2,128)(2,1)S(1)} all-to-all(bf16[2,128,256]{2,0,1:T(2,128)(2,1)S(1)} %copy.10), channel_id=1, replica_groups=mesh['dp'=8,'shard'=128] {'shard'}, dimensions={1} | all-to-all | bytes 262144 | tf_op jit(solution)/shard_map/all_to_all | solution.py:48
  125.4 0.1 multiply_reduce_fusion
  125.6 0.1 divide_convert_fusion
  125.7 0.2 convolution_convert_fusion.4
  125.8 0.3 fusion
  126.2 0.2 convolution_convert_fusion.3
  126.3 0.3 fusion.1
  126.6 0.2 convolution_convert_fusion.2
  126.8 0.3 fusion.2
  127.1 0.2 convolution_convert_fusion.1
  127.2 0.3 fusion.3
  127.6 0.2 convolution_convert_fusion
  127.7 0.3 fusion.7
  128.0 0.1 reshape.39
  128.1 25.4 %copy.12 = bf16[2,1,32768]{0,1,2:T(2,128)(2,1)} copy(bf16[2,1,32768]{2,0,1:T(2,128)(2,1)S(1)} %reshape.39) | data formatting | bytes 262144 | tf_op jit(solution)/shard_map/reshape | solution.py:51
  153.5 0.5 broadcast.75
  154.0 179.1 %reduce.3 = bf16[32768,2]{1,0:T(8,128)(2,1)} reduce(bf16[32768,1,2]{2,1,0:T(2,128)(2,1)} %bitcast.38, bf16[]{:T(256)} %broadcast.75), dimensions={1}, to_apply=%bitcast.10.reduce_sub_computation | reduce | bytes 262146
  333.2 13.1 %reshape.43 = bf16[128,2,256]{2,1,0:T(2,128)(2,1)S(1)} reshape(bf16[32768,2]{1,0:T(8,128)(2,1)} %reduce.3) | data formatting | bytes 262144
  346.2 39.2 %all_to_all.9 = bf16[128,2,256]{2,1,0:T(2,128)(2,1)S(1)} all-to-all(bf16[128,2,256]{2,1,0:T(2,128)(2,1)S(1)} %reshape.43), channel_id=1, replica_groups=mesh['dp'=8,'shard'=128] {'shard'}, dimensions={0} | all-to-all | bytes 262144 | tf_op jit(solution)/shard_map/all_to_all | solution.py:50
  385.4 32.6 %reshape.44 = bf16[32768,1,2]{2,1,0:T(2,128)(2,1)} reshape(bf16[128,2,256]{2,1,0:T(2,128)(2,1)S(1)} %all_to_all.9) | data formatting | bytes 262144
  418.0 30.6 %copy.13 = bf16[2,1,32768]{2,0,1:T(2,128)(2,1)S(1)} copy(bf16[2,1,32768]{0,1,2:T(2,128)(2,1)} %bitcast.39) | data formatting | bytes 262144 | tf_op jit(solution)/shard_map/all_to_all | solution.py:50
  448.5 0.1 reshape.40
  448.6 0.6 slice.4
  (4 shorter events, 0.1 us)
Async XLA Ops:
  7.2 58.5 %reduce-scatter.2.cloned.1.call-start = ((), (), s32[]{:S(2)}) async-start(), calls=%async_computation.3 | async-start | bytes 1548288 | tf_op jit(solution)/shard_map/reduce_scatter | solution.py:67
Sparse Core Ops, SparseCore 0:
  11.4 54.1 reduce-scatter.1
where the time goes:
time: 457 us; the launch traced here: 456 us
  other arithmetic  181 us (40%)
  local copies, waits for them, and re-layouts  103 us (23%)
  blocking collectives  97 us (21%)
  waiting for transfers between devices  58.4 us (13%)
  between operations  14.1 us (3%)
    unnamed x1, other arithmetic  179 us
    all_to_all x1, blocking collectives, orthogonalize(): lax.all_to_all(outgoing, 'shard', split_axis=1, concat_axis=2, tiled=True)  57.9 us
    reduce_scatter x1, waiting for transfers between devices, shards(): lax.psum_scatter(gradients, 'dp', scatter_dimension=2, tiled=True)[0]  57.8 us
    unnamed x3, local copies, waits for them, and re-layouts  46.1 us
    all_to_all x1, blocking collectives, orthogonalize(): lax.all_to_all(results.reshape(capacity, 1, BR * C), 'shard', split_axis=...  39.2 us
    all_to_all x1, local copies, waits for them, and re-layouts, orthogonalize(): lax.all_to_all(results.reshape(capacity, 1, BR * C), 'shard', split_axis=...  30.6 us
    reshape x2, local copies, waits for them, and re-layouts, orthogonalize(): results.reshape(capacity, 1, BR * C)  25.5 us
  transfers between devices with their start and end apart: 1, of which 1 were waited for; matrix products, arithmetic and copies ran while one was open for 0% of the time, Pallas kernels for 0%

commit v1 on v0

v1 whole, which is shorter than its diff:
```python
import jax
import jax.numpy as jnp
from jax import lax
from jax.experimental import pallas as pl
from jax.experimental.pallas import tpu as pltpu
from jax.sharding import PartitionSpec as P

R = 7168
C = 2048
ITERS = 5
BR = 16

COEF_A = 3.4445
COEF_B = -4.775
COEF_C = 2.0315
DECAY = 0.95
EPSILON = 1e-07
ROW_SCALE = 0.2

F32 = jnp.float32
BF16 = jnp.bfloat16
GROUP = 8
HALVES = 2
SLOTS = GROUP * HALVES


def dot(a, b):
    return jnp.dot(a, b, preferred_element_type=F32)


def split(a):
    high = a.astype(BF16)
    rest = a - high.astype(F32)
    middle = rest.astype(BF16)
    low = (rest - middle.astype(F32)).astype(BF16)
    return high, middle, low


def same_block(size):
    rows = lax.broadcasted_iota(jnp.int32, (size, size), 0)
    columns = lax.broadcasted_iota(jnp.int32, (size, size), 1)
    return rows % GROUP == columns % GROUP


def half_of(rows_ref, half):
    wide = rows_ref[...].astype(F32)
    width = wide.shape[-1]
    return wide.reshape(BR, HALVES, GROUP, width)[:, half].reshape(BR * GROUP, width)


def gram_kernel(rows_ref, gram_ref):
    size = BR * GROUP
    mask = same_block(size)
    for half in range(HALVES):
        rows = half_of(rows_ref, half).astype(BF16)
        full = lax.dot_general(rows, rows, (((1,), (1,)), ((), ())), preferred_element_type=F32)
        full = jnp.where(mask, full, 0.0)
        part = jnp.sum(full.reshape(BR, GROUP, size), axis=1)
        for peer in range(gram_ref.shape[0]):
            gram_ref[peer, half] = part


def sweep_kernel(grams_ref, rows_ref, out_ref):
    size = BR * GROUP
    mask = same_block(size)
    same = lax.broadcasted_iota(jnp.int32, (size, size), 0) == lax.broadcasted_iota(jnp.int32, (size, size), 1)
    results = []
    for half in range(HALVES):
        gram = jnp.sum(grams_ref[:, half], axis=0)
        width = gram.shape[-1]
        full = jnp.broadcast_to(gram[:, None, :], (BR, GROUP, width)).reshape(size, size)
        full = jnp.where(mask, full, 0.0)
        diagonal = jnp.where(same, full, 0.0)
        by_column = jnp.sum(diagonal, axis=0, keepdims=True)
        squares = jnp.sum(jnp.where(mask, by_column, 0.0), axis=1, keepdims=True)
        norm = jnp.sqrt(squares) + EPSILON
        inverse = 1.0 / norm
        wide_gram = full * (inverse * inverse)
        current = (half_of(rows_ref, half) / norm).astype(BF16)
        for sweep_index in range(ITERS):
            high, middle, low = split(wide_gram)
            squared = dot(high, high)
            polynomial = (COEF_B * high.astype(F32) + COEF_C * squared).astype(BF16)
            current = (COEF_A * current.astype(F32) + dot(polynomial, current)).astype(BF16)
            if sweep_index + 1 < ITERS:
                left = COEF_A * wide_gram + (dot(polynomial, low) + dot(polynomial, middle) + dot(polynomial, high))
                high, middle, low = split(left)
                wide_gram = COEF_A * left + (dot(low, polynomial) + dot(middle, polynomial) + dot(high, polynomial))
        factor = ROW_SCALE * (float(R) ** 0.5)
        results.append((current.astype(F32) * factor).reshape(BR, 1, GROUP, -1))
    out_ref[...] = jnp.concatenate(results, axis=1).reshape(out_ref.shape).astype(BF16)


def vmem_call(kernel, shape, dtype, count, flops):
    return pl.pallas_call(
        kernel,
        out_shape=jax.ShapeDtypeStruct(shape, dtype),
        in_specs=[pl.BlockSpec(memory_space=pltpu.VMEM)] * count,
        out_specs=pl.BlockSpec(memory_space=pltpu.VMEM),
        cost_estimate=pl.CostEstimate(flops=flops, bytes_accessed=0, transcendentals=0),
    )


def owner_groups():
    chunks = C // 256
    return [[row * chunks + chunk for row in range(BR)] for chunk in range(chunks)]


def chunk_groups():
    chunks = C // 256
    return [[row * chunks + chunk for chunk in range(chunks)] for row in range(BR)]


def gather_sum(gradients):
    groups = lax.axis_size("dp")
    mats, blocks, width = gradients.shape
    parts = gradients.astype(BF16).reshape(mats, groups, blocks // groups, width).swapaxes(0, 1)
    arrived = lax.all_to_all(parts, "dp", 0, 0, tiled=True)
    return jnp.sum(arrived.astype(F32), axis=0)


def shards(gradients, momentum):
    mats, local, width = momentum.shape
    count = mats * local
    summed = gather_sum(gradients[0])
    momentum_next = DECAY * momentum + summed
    nesterov = (summed + DECAY * momentum_next).astype(BF16).reshape(count, width)
    padded = jnp.pad(nesterov, ((0, HALVES * BR * GROUP - count), (0, 0)))
    outgoing = padded.reshape(HALVES, BR, GROUP, width).swapaxes(0, 1).reshape(BR, SLOTS, width)
    rows = lax.all_to_all(outgoing, "shard", 0, 0, tiled=True, axis_index_groups=owner_groups())
    rows = rows.reshape(BR * SLOTS, width)
    chunks = C // width
    parts = vmem_call(gram_kernel, (chunks, HALVES, BR, BR * GROUP), F32, 1, 0)(rows)
    grams = lax.all_to_all(parts, "shard", 0, 0, tiled=True, axis_index_groups=chunk_groups())
    finished = vmem_call(sweep_kernel, rows.shape, BF16, 2, 0)(grams, rows)
    returned = lax.all_to_all(
        finished.reshape(BR, SLOTS, width), "shard", 0, 0, tiled=True, axis_index_groups=owner_groups()
    )
    flat = returned.reshape(BR, HALVES, GROUP, width).swapaxes(0, 1).reshape(HALVES * BR * GROUP, width)
    return momentum_next, flat[:count].reshape(momentum.shape)


def solution(mesh):
    placed = (P("dp", None, None, "shard"), P(None, "dp", "shard"))
    return jax.shard_map(
        shards,
        mesh=mesh,
        in_specs=placed,
        out_specs=(P(None, "dp", "shard"), P(None, "dp", "shard")),
        check_vma=False,
    )
```

time: 457 us -> 126 us (0.28)
  the two profiles are of different devices: /device:TPU:38 before, /device:TPU:96 now
where the time goes in v1:
time: 126 us
  blocking collectives  115 us (91%)
  Pallas kernels  7.55 us (6%)
  other arithmetic  2.21 us (2%)
    all_to_all x1, blocking collectives, shards(): lax.all_to_all(outgoing, 'shard', 0, 0, tiled=True, axis_index_groups=own...  54.6 us
    all_to_all x1, blocking collectives, shards(): lax.all_to_all(finished.reshape(BR, SLOTS, width), 'shard', 0, 0, tiled=T...  32.3 us
    all_to_all x1, blocking collectives, gather_sum(): arrived = lax.all_to_all(parts, 'dp', 0, 0, tiled=True)  16.4 us
    all_to_all x1, blocking collectives, shards(): lax.all_to_all(parts, 'shard', 0, 0, tiled=True, axis_index_groups=chunk_...  11.3 us
    pallas_call x1, Pallas kernels, shards(): finished = vmem_call(sweep_kernel, rows.shape, BF16, 2, 0)(grams, rows)  5.78 us

profile of v1, /device:TPU:96, one launch (start us, length us, event | category | flops | bytes accessed | tf_op | source)
XLA Modules:
  0.0 125.7 jit_solution(12171258592094963144)
XLA Ops:
  0.6 1.4 %convert_element_type.15 = bf16[1,3,448,256]{3,2,1,0:T(8,128)(2,1)S(1)} convert(f32[1,3,448,256]{3,2,1,0:T(8,128)} %param.2) | non-fusion elementwise | flops 344064 | bytes 2064384 | tf_op jit(solution)/shard_map/convert_element_type | solution.py:117
  2.1 0.0 copy-start
  2.1 16.4 %all_to_all.20 = bf16[8,3,56,256]{3,2,1,0:T(8,128)(2,1)S(1)} all-to-all(bf16[8,3,56,256]{3,2,1,0:T(8,128)(2,1)S(1)} %copy.8), channel_id=1, replica_groups=mesh['dp'=8,'shard'=128] {'dp'}, dimensions={0} | all-to-all | bytes 1376256 | tf_op jit(solution)/shard_map/all_to_all | solution.py:118
  18.5 0.1 convert_reduce_fusion
  18.6 0.0 copy-done
  18.6 0.7 add_convert_fusion
  19.3 54.6 %all_to_all.21 = bf16[16,16,256]{2,1,0:T(8,128)(2,1)} all-to-all(bf16[16,16,256]{2,1,0:T(8,128)(2,1)S(1)} %bitcast.22), channel_id=1, replica_groups={{0,8,16,24,32,40,48,56,64,72,80,88,96,104,112,120},{1,9,17,25,33,41,49,..., dimensions={0} | all-to-all | bytes 262144 | tf_op jit(solution)/shard_map/all_to_all | solution.py:130
  74.0 1.8 %shard_map.41 = f32[8,2,16,128]{3,2,1,0:T(8,128)} custom-call(bf16[256,256]{1,0:T(8,128)(2,1)} %bitcast.18), custom_call_target="tpu_custom_call" | custom-call | tf_op jit(solution)/shard_map/pallas_call | solution.py:133
  75.7 11.3 %all_to_all.22.grams_ref = f32[8,2,16,128]{3,2,1,0:T(8,128)} all-to-all(f32[8,2,16,128]{3,2,1,0:T(8,128)} %shard_map.41), channel_id=1, replica_groups={{0,1,2,3,4,5,6,7},{8,9,10,11,12,13,14,15},{16,17,18,19,20,21,22,23},{24..., dimensions={0} | all-to-all | bytes 262144 | tf_op jit(solution)/shard_map/all_to_all | solution.py:134
  87.0 5.8 %shard_map.42 = bf16[256,256]{1,0:T(8,128)(2,1)} custom-call(f32[8,2,16,128]{3,2,1,0:T(8,128)} %all_to_all.22.grams_ref, bf16[256,256]{1,0:T(8,128)(2,1)} %bitcast.19), custom_call_target="tpu_custom_call" | custom-call | tf_op jit(solution)/shard_map/pallas_call | solution.py:135
  92.8 32.3 %all_to_all.23 = bf16[16,16,256]{2,1,0:T(8,128)(2,1)S(1)} all-to-all(bf16[16,16,256]{2,1,0:T(8,128)(2,1)} %bitcast.20), channel_id=1, replica_groups={{0,8,16,24,32,40,48,56,64,72,80,88,96,104,112,120},{1,9,17,25,33,41,49,..., dimensions={0} | all-to-all | bytes 262144 | tf_op jit(solution)/shard_map/all_to_all | solution.py:136
  125.1 0.6 slice.4
  (4 shorter events, 0.1 us)
Async XLA Ops:
  2.1 16.5 %copy-start = (f32[3,56,256]{2,1,0:T(8,128)S(1)}, f32[3,56,256]{2,1,0:T(8,128)}, u32[]{:S(2)}) copy-start(f32[3,56,256]{2,1,0:T(8,128)} %param.3) | copy-start | bytes 516100

commit v2 on v1

v2 whole, which is shorter than its diff:
```python
import jax
import jax.numpy as jnp
from jax import lax
from jax.experimental import pallas as pl
from jax.experimental.pallas import tpu as pltpu
from jax.sharding import PartitionSpec as P

R = 7168
C = 2048
ITERS = 5
BR = 16

COEF_A = 3.4445
COEF_B = -4.775
COEF_C = 2.0315
DECAY = 0.95
EPSILON = 1e-07
ROW_SCALE = 0.2

F32 = jnp.float32
BF16 = jnp.bfloat16
LANES = 128
GROUP = 8
HALF = GROUP // 2
SIZE = BR * GROUP
TILES = 3


def dot(a, b):
    return jnp.dot(a, b, preferred_element_type=F32)


def split(a):
    high = a.astype(BF16)
    return high, (a - high.astype(F32)).astype(BF16)


def pack(rows):
    owners = BR
    count, width = rows.shape
    first = owners * GROUP
    halves = rows[:first].reshape(owners, GROUP, 2, LANES).swapaxes(1, 2)
    others = rows[first:].reshape((count - first) // HALF, HALF, 2, LANES).swapaxes(1, 2)
    others = others.reshape(-1, 1, GROUP, LANES)
    others = jnp.pad(others, ((0, owners - others.shape[0]), (0, 0), (0, 0), (0, 0)))
    return jnp.concatenate([halves, others], axis=1)


def unpack(tiles, count):
    owners = BR
    first = owners * GROUP
    halves = tiles[:, :2].swapaxes(1, 2).reshape(first, 2 * LANES)
    others = tiles[: (count - first) // HALF, 2].reshape(-1, 2, HALF, LANES).swapaxes(1, 2)
    return jnp.concatenate([halves, others.reshape(count - first, 2 * LANES)], axis=0)


def row_groups(rows_ref):
    wide = rows_ref[...].astype(F32)
    tiles = [wide[:, tile].reshape(SIZE, LANES) for tile in range(TILES)]
    return [jnp.concatenate(tiles[:2], axis=1), tiles[2]]


def same_slot():
    rows = lax.broadcasted_iota(jnp.int32, (SIZE, SIZE), 0)
    columns = lax.broadcasted_iota(jnp.int32, (SIZE, SIZE), 1)
    return rows % GROUP == columns % GROUP


def gram_kernel(rows_ref, gram_ref):
    mask = same_slot()
    parts = []
    for rows in row_groups(rows_ref):
        rows = rows.astype(BF16)
        full = lax.dot_general(rows, rows, (((1,), (1,)), ((), ())), preferred_element_type=F32)
        parts.append(jnp.sum(jnp.where(mask, full, 0.0).reshape(BR, GROUP, SIZE), axis=1))
    halves = parts[1]
    lane = lax.broadcasted_iota(jnp.int32, halves.shape, 1)
    other = jnp.where(lane % GROUP < HALF, pltpu.roll(halves, SIZE - HALF, 1), pltpu.roll(halves, HALF, 1))
    parts[1] = halves + other
    for peer in range(gram_ref.shape[0]):
        for group, part in enumerate(parts):
            gram_ref[peer, group] = part


def sweep_kernel(grams_ref, rows_ref, out_ref):
    mask = same_slot()
    same = lax.broadcasted_iota(jnp.int32, (SIZE, SIZE), 0) == lax.broadcasted_iota(jnp.int32, (SIZE, SIZE), 1)
    grams = []
    currents = []
    for group, rows in enumerate(row_groups(rows_ref)):
        gram = jnp.sum(grams_ref[:, group], axis=0)
        full = jnp.broadcast_to(gram[:, None, :], (BR, GROUP, SIZE)).reshape(SIZE, SIZE)
        full = jnp.where(mask, full, 0.0)
        by_column = jnp.sum(jnp.where(same, full, 0.0), axis=0, keepdims=True)
        squares = jnp.sum(jnp.where(mask, by_column, 0.0), axis=1, keepdims=True)
        norm = jnp.sqrt(squares) + EPSILON
        inverse = 1.0 / norm
        grams.append(full * (inverse * inverse))
        currents.append((rows / norm).astype(BF16))
    for sweep_index in range(ITERS):
        parts = [split(gram) for gram in grams]
        squared = [dot(part[0], part[0]) for part in parts]
        polynomials = [
            (COEF_B * part[0].astype(F32) + COEF_C * square).astype(BF16) for part, square in zip(parts, squared)
        ]
        if sweep_index + 1 < ITERS:
            lefts = [
                COEF_A * gram + (dot(poly, part[1]) + dot(poly, part[0]))
                for gram, poly, part in zip(grams, polynomials, parts)
            ]
        currents = [
            (COEF_A * current.astype(F32) + dot(poly, current)).astype(BF16)
            for current, poly in zip(currents, polynomials)
        ]
        if sweep_index + 1 < ITERS:
            parts = [split(left) for left in lefts]
            grams = [
                COEF_A * left + (dot(part[1], poly) + dot(part[0], poly))
                for left, poly, part in zip(lefts, polynomials, parts)
            ]
    factor = ROW_SCALE * (float(R) ** 0.5)
    first, second = [(current.astype(F32) * factor) for current in currents]
    tiles = [first[:, :LANES], first[:, LANES:], second]
    tiles = [tile.reshape(BR, 1, GROUP, LANES) for tile in tiles]
    out_ref[...] = jnp.concatenate(tiles, axis=1).astype(BF16)


def vmem_call(kernel, shape, dtype, count, flops):
    return pl.pallas_call(
        kernel,
        out_shape=jax.ShapeDtypeStruct(shape, dtype),
        in_specs=[pl.BlockSpec(memory_space=pltpu.VMEM)] * count,
        out_specs=pl.BlockSpec(memory_space=pltpu.VMEM),
        compiler_params=pltpu.CompilerParams(vmem_limit_bytes=4 << 20),
        cost_estimate=pl.CostEstimate(flops=flops, bytes_accessed=0, transcendentals=0),
    )


def owner_groups():
    chunks = C // 256
    return [[(row * 5 + 8) % BR * chunks + chunk for row in range(BR)] for chunk in range(chunks)]


def chunk_groups():
    chunks = C // 256
    return [[row * chunks + (chunk ^ 2) for chunk in range(chunks)] for row in range(BR)]


def gather_sum(gradients):
    groups = lax.axis_size("dp")
    mats, blocks, width = gradients.shape
    parts = gradients.astype(BF16).reshape(mats, groups, blocks // groups, width).swapaxes(0, 1)
    arrived = lax.all_to_all(parts, "dp", 0, 0, tiled=True)
    return jnp.sum(arrived.astype(F32), axis=0)


def shards(gradients, momentum):
    mats, local, width = momentum.shape
    count = mats * local
    summed = gather_sum(gradients[0])
    momentum_next = DECAY * momentum + summed
    nesterov = (summed + DECAY * momentum_next).astype(BF16).reshape(count, width)
    outgoing = pack(nesterov)
    rows = lax.all_to_all(outgoing, "shard", 0, 0, tiled=True, axis_index_groups=owner_groups())
    chunks = C // width
    parts = vmem_call(gram_kernel, (chunks, 2, BR, SIZE), F32, 1, 0)(rows)
    grams = lax.all_to_all(parts, "shard", 0, 0, tiled=True, axis_index_groups=chunk_groups())
    finished = vmem_call(sweep_kernel, rows.shape, BF16, 2, 0)(grams, rows)
    returned = lax.all_to_all(finished, "shard", 0, 0, tiled=True, axis_index_groups=owner_groups())
    return momentum_next, unpack(returned, count).reshape(momentum.shape)


def solution(mesh):
    placed = (P("dp", None, None, "shard"), P(None, "dp", "shard"))
    return jax.shard_map(
        shards,
        mesh=mesh,
        in_specs=placed,
        out_specs=(P(None, "dp", "shard"), P(None, "dp", "shard")),
        check_vma=False,
    )
```

time: 126 us -> 104 us (0.83)
  the two profiles are of different devices: /device:TPU:96 before, /device:TPU:8 now
where the time goes in v2:
time: 104 us
  blocking collectives  97.9 us (94%)
  other arithmetic  2.86 us (3%)
  Pallas kernels  2.4 us (2%)
    all_to_all x1, blocking collectives, shards(): lax.all_to_all(outgoing, 'shard', 0, 0, tiled=True, axis_index_groups=own...  43.6 us
    all_to_all x1, blocking collectives, shards(): lax.all_to_all(finished, 'shard', 0, 0, tiled=True, axis_index_groups=own...  27.7 us
    all_to_all x1, blocking collectives, gather_sum(): arrived = lax.all_to_all(parts, 'dp', 0, 0, tiled=True)  16.4 us
    all_to_all x1, blocking collectives, shards(): lax.all_to_all(parts, 'shard', 0, 0, tiled=True, axis_index_groups=chunk_...  10.2 us
    pallas_call x1, Pallas kernels, shards(): finished = vmem_call(sweep_kernel, rows.shape, BF16, 2, 0)(grams, rows)  2.15 us

profile of v2, /device:TPU:8, one launch (start us, length us, event | category | flops | bytes accessed | tf_op | source)
XLA Modules:
  0.0 104.0 jit_solution(3305030591222714409)
XLA Ops:
  0.6 1.4 %convert_element_type.15 = bf16[1,3,448,256]{3,2,1,0:T(8,128)(2,1)S(1)} convert(f32[1,3,448,256]{3,2,1,0:T(8,128)} %param.2) | non-fusion elementwise | flops 344064 | bytes 2064384 | tf_op jit(solution)/shard_map/convert_element_type | solution.py:152
  2.1 0.0 copy-start
  2.1 16.4 %all_to_all.20 = bf16[8,3,56,256]{3,2,1,0:T(8,128)(2,1)S(1)} all-to-all(bf16[8,3,56,256]{3,2,1,0:T(8,128)(2,1)S(1)} %copy.8), channel_id=1, replica_groups=mesh['dp'=8,'shard'=128] {'dp'}, dimensions={0} | all-to-all | bytes 1376256 | tf_op jit(solution)/shard_map/all_to_all | solution.py:153
  18.5 0.1 convert_reduce_fusion
  18.6 0.0 copy-done
  18.6 0.7 add_convert_fusion
  19.4 43.6 %all_to_all.21.rows_ref = bf16[16,3,8,128]{3,2,1,0:T(8,128)(2,1)S(1)} all-to-all(bf16[16,3,8,128]{3,2,1,0:T(8,128)(2,1)S(1)} %fusion.1), channel_id=1, replica_groups={{64,104,16,56,96,8,48,88,0,40,80,120,32,72,112,24},{65,105,17,57,97,9,4..., dimensions={0} | all-to-all | bytes 196608 | tf_op jit(solution)/shard_map/all_to_all | solution.py:164
  62.9 0.2 shard_map.41
  63.2 10.2 %all_to_all.22.grams_ref = f32[8,2,16,128]{3,2,1,0:T(8,128)S(1)} all-to-all(f32[8,2,16,128]{3,2,1,0:T(8,128)S(1)} %shard_map.41), channel_id=1, replica_groups={{2,3,0,1,6,7,4,5},{10,11,8,9,14,15,12,13},{18,19,16,17,22,23,20,21},{26..., dimensions={0} | all-to-all | bytes 262144 | tf_op jit(solution)/shard_map/all_to_all | solution.py:167
  73.4 2.2 %shard_map.42 = bf16[16,3,8,128]{3,2,1,0:T(8,128)(2,1)S(1)} custom-call(f32[8,2,16,128]{3,2,1,0:T(8,128)S(1)} %all_to_all.22.grams_ref, bf16[16,3,8,128]{3,2,1,0:T(8,128)(2,1)S(1)} %all_to_all.21.rows_ref), custom_call_target="tpu_custom_call" | custom-call | tf_op jit(solution)/shard_map/pallas_call | solution.py:168
  75.5 27.7 %all_to_all.23 = bf16[16,3,8,128]{3,2,1,0:T(8,128)(2,1)S(1)} all-to-all(bf16[16,3,8,128]{3,2,1,0:T(8,128)(2,1)S(1)} %shard_map.42), channel_id=1, replica_groups={{64,104,16,56,96,8,48,88,0,40,80,120,32,72,112,24},{65,105,17,57,97,9,4..., dimensions={0} | all-to-all | bytes 196608 | tf_op jit(solution)/shard_map/all_to_all | solution.py:169
  103.3 0.6 pad_maximum_fusion
  (10 shorter events, 0.1 us)
Async XLA Ops:
  2.1 16.5 %copy-start = (f32[3,56,256]{2,1,0:T(8,128)S(1)}, f32[3,56,256]{2,1,0:T(8,128)}, u32[]{:S(2)}) copy-start(f32[3,56,256]{2,1,0:T(8,128)} %param.3) | copy-start | bytes 516100

commit v3 on v2

--- a/solution.py
+++ b/solution.py
@@ -19,11 +19,13 @@
 
 F32 = jnp.float32
 BF16 = jnp.bfloat16
+CORES = 2
 LANES = 128
 GROUP = 8
 HALF = GROUP // 2
 SIZE = BR * GROUP
-TILES = 3
+REST = 3
+SENT = 2 * (GROUP + REST)
 
 
 def dot(a, b):
@@ -39,24 +41,32 @@
     owners = BR
     count, width = rows.shape
     first = owners * GROUP
-    halves = rows[:first].reshape(owners, GROUP, 2, LANES).swapaxes(1, 2)
-    others = rows[first:].reshape((count - first) // HALF, HALF, 2, LANES).swapaxes(1, 2)
-    others = others.reshape(-1, 1, GROUP, LANES)
-    others = jnp.pad(others, ((0, owners - others.shape[0]), (0, 0), (0, 0), (0, 0)))
-    return jnp.concatenate([halves, others], axis=1)
-
-
-def unpack(tiles, count):
+    halves = rows[:first].reshape(owners, GROUP, 2, LANES).swapaxes(1, 2).reshape(owners, 2 * GROUP, LANES)
+    others = jnp.pad(rows[first:], ((0, first + owners * REST - count), (0, 0)))
+    others = others.reshape(owners, REST, 2, LANES).swapaxes(1, 2).reshape(owners, 2 * REST, LANES)
+    return jnp.concatenate([halves, others], axis=1).reshape(owners, -1, 2, LANES)
+
+
+def unpack(pairs, count):
     owners = BR
     first = owners * GROUP
-    halves = tiles[:, :2].swapaxes(1, 2).reshape(first, 2 * LANES)
-    others = tiles[: (count - first) // HALF, 2].reshape(-1, 2, HALF, LANES).swapaxes(1, 2)
-    return jnp.concatenate([halves, others.reshape(count - first, 2 * LANES)], axis=0)
+    tiles = pairs.reshape(owners, -1, LANES)
+    halves = tiles[:, : 2 * GROUP].reshape(owners, 2, GROUP, LANES).swapaxes(1, 2).reshape(first, 2 * LANES)
+    others = tiles[:, 2 * GROUP :].reshape(owners, 2, REST, LANES).swapaxes(1, 2).reshape(-1, 2 * LANES)
+    return jnp.concatenate([halves, others[: count - first]], axis=0)
 
 
 def row_groups(rows_ref):
     wide = rows_ref[...].astype(F32)
-    tiles = [wide[:, tile].reshape(SIZE, LANES) for tile in range(TILES)]
+    empty = jnp.zeros((HALF - REST, LANES), F32)
+    tiles = [[], [], []]
+    for row in range(BR):
+        base = row * SENT
+        tiles[0].append(wide[base : base + GROUP])
+        tiles[1].append(wide[base + GROUP : base + 2 * GROUP])
+        base += 2 * GROUP
+        tiles[2] += [wide[base : base + REST], empty, wide[base + REST : base + 2 * REST], empty]
+    tiles = [jnp.concatenate(tile, axis=0) for tile in tiles]
     return [jnp.concatenate(tiles[:2], axis=1), tiles[2]]
 
 
@@ -74,21 +84,34 @@
         full = lax.dot_general(rows, rows, (((1,), (1,)), ((), ())), preferred_element_type=F32)
         parts.append(jnp.sum(jnp.where(mask, full, 0.0).reshape(BR, GROUP, SIZE), axis=1))
     halves = parts[1]
-    lane = lax.broadcasted_iota(jnp.int32, halves.shape, 1)
-    other = jnp.where(lane % GROUP < HALF, pltpu.roll(halves, SIZE - HALF, 1), pltpu.roll(halves, HALF, 1))
-    parts[1] = halves + other
+    low_half = lax.broadcasted_iota(jnp.int32, halves.shape, 1) % GROUP < HALF
+    halves = halves + jnp.where(low_half, pltpu.roll(halves, SIZE - HALF, 1), pltpu.roll(halves, HALF, 1))
+    parts[1] = jnp.where(low_half[:GROUP], halves[:GROUP], halves[GROUP:])
+    packed = jnp.concatenate(parts, axis=0)
     for peer in range(gram_ref.shape[0]):
-        for group, part in enumerate(parts):
-            gram_ref[peer, group] = part
-
-
-def sweep_kernel(grams_ref, rows_ref, out_ref):
+        gram_ref[peer] = packed
+
+
+def unfold(total, group):
+    if group == 0:
+        return total[:BR]
+    folded = total[BR:]
+    low_half = lax.broadcasted_iota(jnp.int32, folded.shape, 1) % GROUP < HALF
+    upper = jnp.where(low_half, folded, pltpu.roll(folded, HALF, 1))
+    lower = jnp.where(low_half, pltpu.roll(folded, SIZE - HALF, 1), folded)
+    return jnp.concatenate([upper, lower], axis=0)
+
+
+def sweep_kernel(grams_ref, rows_ref, momentum_ref, out_ref, momentum_out_ref, done):
+    written = pltpu.make_async_copy(momentum_ref, momentum_out_ref, done)
+    written.start()
     mask = same_slot()
     same = lax.broadcasted_iota(jnp.int32, (SIZE, SIZE), 0) == lax.broadcasted_iota(jnp.int32, (SIZE, SIZE), 1)
+    total = jnp.sum(grams_ref[...], axis=0)
     grams = []
     currents = []
     for group, rows in enumerate(row_groups(rows_ref)):
-        gram = jnp.sum(grams_ref[:, group], axis=0)
+        gram = unfold(total, group)
         full = jnp.broadcast_to(gram[:, None, :], (BR, GROUP, SIZE)).reshape(SIZE, SIZE)
         full = jnp.where(mask, full, 0.0)
         by_column = jnp.sum(jnp.where(same, full, 0.0), axis=0, keepdims=True)
@@ -120,9 +143,13 @@
             ]
     factor = ROW_SCALE * (float(R) ** 0.5)
     first, second = [(current.astype(F32) * factor) for current in currents]
-    tiles = [first[:, :LANES], first[:, LANES:], second]
-    tiles = [tile.reshape(BR, 1, GROUP, LANES) for tile in tiles]
-    out_ref[...] = jnp.concatenate(tiles, axis=1).astype(BF16)
+    pieces = []
+    for row in range(BR):
+        base = row * GROUP
+        pieces += [first[base : base + GROUP, :LANES], first[base : base + GROUP, LANES:]]
+        pieces += [second[base : base + REST], second[base + HALF : base + HALF + REST]]
+    out_ref[...] = jnp.concatenate(pieces, axis=0).astype(BF16)
+    written.wait()
 
 
 def vmem_call(kernel, shape, dtype, count, flops):
@@ -149,8 +176,14 @@
 def gather_sum(gradients):
     groups = lax.axis_size("dp")
     mats, blocks, width = gradients.shape
-    parts = gradients.astype(BF16).reshape(mats, groups, blocks // groups, width).swapaxes(0, 1)
-    arrived = lax.all_to_all(parts, "dp", 0, 0, tiled=True)
+    core = lax.axis_index("dp") % CORES
+    parts = gradients.reshape(mats, groups // CORES, CORES, blocks // groups, width)
+    sent = lax.dynamic_index_in_dim(parts, 1 - core, 2, keepdims=False).astype(BF16)
+    arrived = lax.ppermute(sent, "dp", [(i, i ^ 1) for i in range(groups)])
+    own = lax.optimization_barrier(lax.dynamic_index_in_dim(parts, core, 2, keepdims=False))
+    pair = (own + arrived.astype(F32)).astype(BF16).swapaxes(0, 1)
+    chips = [[chip * CORES + side for chip in range(groups // CORES)] for side in range(CORES)]
+    arrived = lax.all_to_all(pair, "dp", 0, 0, tiled=True, axis_index_groups=chips)
     return jnp.sum(arrived.astype(F32), axis=0)
 
 
@@ -162,12 +195,24 @@
     nesterov = (summed + DECAY * momentum_next).astype(BF16).reshape(count, width)
     outgoing = pack(nesterov)
     rows = lax.all_to_all(outgoing, "shard", 0, 0, tiled=True, axis_index_groups=owner_groups())
+    rows = rows.reshape(BR * SENT, LANES)
     chunks = C // width
-    parts = vmem_call(gram_kernel, (chunks, 2, BR, SIZE), F32, 1, 0)(rows)
+    parts = vmem_call(gram_kernel, (chunks, BR + GROUP, SIZE), F32, 1, 0)(rows)
     grams = lax.all_to_all(parts, "shard", 0, 0, tiled=True, axis_index_groups=chunk_groups())
-    finished = vmem_call(sweep_kernel, rows.shape, BF16, 2, 0)(grams, rows)
+    finished, momentum_out = pl.pallas_call(
+        sweep_kernel,
+        out_shape=[
+            jax.ShapeDtypeStruct(rows.shape, BF16),
+            jax.ShapeDtypeStruct(momentum.shape, F32),
+        ],
+        in_specs=[pl.BlockSpec(memory_space=pltpu.VMEM)] * 3,
+        out_specs=[pl.BlockSpec(memory_space=pltpu.VMEM), pl.BlockSpec(memory_space=pl.ANY)],
+        scratch_shapes=[pltpu.SemaphoreType.DMA],
+        compiler_params=pltpu.CompilerParams(vmem_limit_bytes=4 << 20),
+    )(grams, rows, momentum_next)
+    finished = finished.reshape(outgoing.shape)
     returned = lax.all_to_all(finished, "shard", 0, 0, tiled=True, axis_index_groups=owner_groups())
-    return momentum_next, unpack(returned, count).reshape(momentum.shape)
+    return momentum_out, unpack(returned, count).reshape(momentum.shape)
 
 
 def solution(mesh):

time: 104 us -> 101 us (0.971)
  blocking collectives: 97.9 us -> 91.3 us
  other arithmetic: 2.86 us -> 0.81 us
  starting transfers between devices: 0 us -> 1.92 us
  waiting for transfers between devices: 0 us -> 1.53 us
  local copies, waits for them, and re-layouts: 0.12 us -> 1.65 us
    all_to_all x1, blocking collectives: 16.4 us -> 11.9 us  [gather_sum(): lax.all_to_all(pair, 'dp', 0, 0, tiled=True, axis_index_groups=chips)]
    convert_element_type x2 -> x0, other arithmetic: 2.12 us -> none  [the longest x1 1.41 us: gather_sum(): gradients.astype(BF16).reshape(mats, groups, blocks // groups, width)]
    ppermute x0 -> x1, starting transfers between devices: none -> 1.92 us  [gather_sum(): arrived = lax.ppermute(sent, 'dp', [(i, i ^ 1) for i in range(groups)])]
    ppermute x0 -> x1, waiting for transfers between devices: none -> 1.53 us  [gather_sum(): arrived = lax.ppermute(sent, 'dp', [(i, i ^ 1) for i in range(groups)])]
    unnamed x3 -> x5, local copies, waits for them, and re-layouts: 0.01 us -> 1.33 us
    all_to_all x1, blocking collectives: 43.6 us -> 42.3 us  [shards(): lax.all_to_all(outgoing, 'shard', 0, 0, tiled=True, axis_index_groups=own...]
  transfers between devices with their start and end apart: 0 -> 1, of which waited for: 0 -> 1; matrix products, arithmetic and copies ran while one was open for 0% -> 0% of each run, Pallas kernels for 0% -> 0%
where the time goes in v3:
time: 101 us; the launch traced here: 100 us
  blocking collectives  91.3 us (90%)
  Pallas kernels  2.38 us (2%)
  starting transfers between devices  1.92 us (2%)
  local copies, waits for them, and re-layouts  1.65 us (2%)
  waiting for transfers between devices  1.53 us (2%)
    all_to_all x1, blocking collectives, shards(): lax.all_to_all(outgoing, 'shard', 0, 0, tiled=True, axis_index_groups=own...  42.3 us
    all_to_all x1, blocking collectives, shards(): lax.all_to_all(finished, 'shard', 0, 0, tiled=True, axis_index_groups=own...  27.1 us
    all_to_all x1, blocking collectives, gather_sum(): lax.all_to_all(pair, 'dp', 0, 0, tiled=True, axis_index_groups=chips)  11.9 us
    all_to_all x1, blocking collectives, shards(): lax.all_to_all(parts, 'shard', 0, 0, tiled=True, axis_index_groups=chunk_...  9.99 us
    pallas_call x1, Pallas kernels, shards(): pl.pallas_call(sweep_kernel, out_shape=[jax.ShapeDtypeStruct(rows.shape,...  2.13 us
  transfers between devices with their start and end apart: 1, of which 1 were waited for; matrix products, arithmetic and copies ran while one was open for 0% of the time, Pallas kernels for 0%

profile of v3, /device:TPU:8, one launch (start us, length us, event | category | flops | bytes accessed | tf_op | source)
XLA Modules:
  0.0 100.4 jit_solution(7920504788114872109)
XLA Ops:
  0.6 0.0 copy-start
  0.7 1.3 %copy-done = f32[1,3,448,256]{3,2,1,0:T(8,128)S(1)} copy-done((f32[1,3,448,256]{3,2,1,0:T(8,128)S(1)}, f32[1,3,448,256]{3,2,1,0:T(8,128)}, u32[]{:S(2)}) %copy-start) | copy-done | bytes 1376280
  2.0 1.9 %collective-permute-start = (bf16[3,4,56,256]{3,2,1,0:T(8,128)(2,1)S(1)}, bf16[3,4,56,256]{3,2,1,0:T(8,128)(2,1)S(1)}, u32[]{:S(2)}, u32[]{:S(2)}) collective-permute-start(bf16[3,4,56,256]{3,2,1,0:T(8,128)(2,1)S(1)} %fusion), channel_id=1, source_target_pairs={{0,128},{128,0},{256,384},{384,256},{512,640},{640,512},{768,896},... | collective-permute-start | bytes 1032200 | tf_op jit(solution)/shard_map/ppermute | solution.py:182
  3.9 0.1 dynamic-slice_bitcast_fusion
  4.0 0.0 copy-start.1
  4.0 1.5 %collective-permute-done = bf16[3,4,56,256]{3,2,1,0:T(8,128)(2,1)S(1)} collective-permute-done((bf16[3,4,56,256]{3,2,1,0:T(8,128)(2,1)S(1)}, bf16[3,4,56,256]{3,2,1,0:T(8,128)(2,1)S(1)}, u32[]{:S(2)}, u32[]{:S(2)}) %collective-permute-start) | collective-permute-done | bytes 344096 | tf_op jit(solution)/shard_map/ppermute | solution.py:182
  5.6 0.1 fusion.1
  5.7 11.9 %all_to_all.20 = bf16[4,3,56,256]{3,2,1,0:T(8,128)(2,1)S(1)} all-to-all(bf16[4,3,56,256]{3,2,1,0:T(8,128)(2,1)S(1)} %copy.20), channel_id=1, replica_groups={{0,256,512,768},{128,384,640,896},{1,257,513,769},{129,385,641,897},{2,..., dimensions={0} | all-to-all | bytes 688128 | tf_op jit(solution)/shard_map/all_to_all | solution.py:186
  17.7 0.0 copy-done.1
  17.8 0.1 copy.23
  17.9 42.3 %all_to_all.21 = bf16[16,11,2,128]{3,2,1,0:T(2,128)(2,1)S(1)} all-to-all(bf16[16,11,2,128]{3,2,1,0:T(2,128)(2,1)S(1)} %copy.23), channel_id=1, replica_groups={{64,104,16,56,96,8,48,88,0,40,80,120,32,72,112,24},{65,105,17,57,97,9,4..., dimensions={0} | all-to-all | bytes 180224 | tf_op jit(solution)/shard_map/all_to_all | solution.py:197
  60.2 0.3 shard_map.41
  60.5 10.0 %all_to_all.22.grams_ref = f32[8,24,128]{2,1,0:T(8,128)S(1)} all-to-all(f32[8,24,128]{2,1,0:T(8,128)S(1)} %shard_map.41), channel_id=1, replica_groups={{2,3,0,1,6,7,4,5},{10,11,8,9,14,15,12,13},{18,19,16,17,22,23,20,21},{26..., dimensions={0} | all-to-all | bytes 196608 | tf_op jit(solution)/shard_map/all_to_all | solution.py:201
  70.5 2.1 %shard_map.42 = (bf16[352,128]{1,0:T(8,128)(2,1)S(1)}, f32[3,56,256]{2,1,0:T(8,128)}) custom-call(f32[8,24,128]{2,1,0:T(8,128)S(1)} %all_to_all.22.grams_ref, bf16[352,128]{1,0:T(8,128)(2,1)S(1)} %bitcast.37, f32[3,56,256]{2,1,0:T(8,128)S(1)} %get-tuple-element.6.momentum_ref), custom_call_target="tpu_custom_call" | custom-call | tf_op jit(solution)/shard_map/pallas_call | solution.py:202
  72.6 27.1 %all_to_all.23 = bf16[16,11,2,128]{3,2,1,0:T(2,128)(2,1)S(1)} all-to-all(bf16[16,11,2,128]{3,2,1,0:T(2,128)(2,1)S(1)} %bitcast.38), channel_id=1, replica_groups={{64,104,16,56,96,8,48,88,0,40,80,120,32,72,112,24},{65,105,17,57,97,9,4..., dimensions={0} | all-to-all | bytes 180224 | tf_op jit(solution)/shard_map/all_to_all | solution.py:214
  99.8 0.6 pad_maximum_fusion.1
  (18 shorter events, 0.3 us)
Async XLA Ops:
  0.6 1.3 %copy-start = (f32[1,3,448,256]{3,2,1,0:T(8,128)S(1)}, f32[1,3,448,256]{3,2,1,0:T(8,128)}, u32[]{:S(2)}) copy-start(f32[1,3,448,256]{3,2,1,0:T(8,128)} %param.2) | copy-start | bytes 4128772
  2.0 3.5 %collective-permute-start = (bf16[3,4,56,256]{3,2,1,0:T(8,128)(2,1)S(1)}, bf16[3,4,56,256]{3,2,1,0:T(8,128)(2,1)S(1)}, u32[]{:S(2)}, u32[]{:S(2)}) collective-permute-start(bf16[3,4,56,256]{3,2,1,0:T(8,128)(2,1)S(1)} %fusion), channel_id=1, source_target_pairs={{0,128},{128,0},{256,384},{384,256},{512,640},{640,512},{768,896},... | collective-permute-start | bytes 1032200 | tf_op jit(solution)/shard_map/ppermute | solution.py:182
  4.0 13.6 %copy-start.1 = (f32[3,56,256]{2,1,0:T(8,128)S(1)}, f32[3,56,256]{2,1,0:T(8,128)}, u32[]{:S(2)}) copy-start(f32[3,56,256]{2,1,0:T(8,128)} %param.3) | copy-start | bytes 516100

commit v4 on v3

--- a/solution.py
+++ b/solution.py
@@ -128,7 +128,7 @@
         ]
         if sweep_index + 1 < ITERS:
             lefts = [
-                COEF_A * gram + (dot(poly, part[1]) + dot(poly, part[0]))
+                COEF_A * gram + dot(jnp.concatenate([poly, poly], axis=1), jnp.concatenate(part, axis=0))
                 for gram, poly, part in zip(grams, polynomials, parts)
             ]
         currents = [
@@ -138,7 +138,7 @@
         if sweep_index + 1 < ITERS:
             parts = [split(left) for left in lefts]
             grams = [
-                COEF_A * left + (dot(part[1], poly) + dot(part[0], poly))
+                COEF_A * left + dot(jnp.concatenate(part, axis=1), jnp.concatenate([poly, poly], axis=0))
                 for left, poly, part in zip(lefts, polynomials, parts)
             ]
     factor = ROW_SCALE * (float(R) ** 0.5)
@@ -180,8 +180,9 @@
     parts = gradients.reshape(mats, groups // CORES, CORES, blocks // groups, width)
     sent = lax.dynamic_index_in_dim(parts, 1 - core, 2, keepdims=False).astype(BF16)
     arrived = lax.ppermute(sent, "dp", [(i, i ^ 1) for i in range(groups)])
-    own = lax.optimization_barrier(lax.dynamic_index_in_dim(parts, core, 2, keepdims=False))
-    pair = (own + arrived.astype(F32)).astype(BF16).swapaxes(0, 1)
+    _, again = lax.optimization_barrier((sent, parts))
+    own = lax.optimization_barrier(lax.dynamic_index_in_dim(again, core, 2, keepdims=False).astype(BF16))
+    pair = (own.astype(F32) + arrived.astype(F32)).astype(BF16).swapaxes(0, 1)
     chips = [[chip * CORES + side for chip in range(groups // CORES)] for side in range(CORES)]
     arrived = lax.all_to_all(pair, "dp", 0, 0, tiled=True, axis_index_groups=chips)
     return jnp.sum(arrived.astype(F32), axis=0)

time: 101 us -> 101 us (level)
  no operation moved by 1% of the time
where the time goes in v4:
time: 101 us; the launch traced here: 100 us
  blocking collectives  91.3 us (90%)
  Pallas kernels  2.31 us (2%)
  starting transfers between devices  1.92 us (2%)
  local copies, waits for them, and re-layouts  1.63 us (2%)
  waiting for transfers between devices  1.55 us (2%)
    all_to_all x1, blocking collectives, shards(): lax.all_to_all(outgoing, 'shard', 0, 0, tiled=True, axis_index_groups=own...  42.3 us
    all_to_all x1, blocking collectives, shards(): lax.all_to_all(finished, 'shard', 0, 0, tiled=True, axis_index_groups=own...  27.1 us
    all_to_all x1, blocking collectives, gather_sum(): lax.all_to_all(pair, 'dp', 0, 0, tiled=True, axis_index_groups=chips)  11.9 us
    all_to_all x1, blocking collectives, shards(): lax.all_to_all(parts, 'shard', 0, 0, tiled=True, axis_index_groups=chunk_...  9.99 us
    pallas_call x1, Pallas kernels, shards(): pl.pallas_call(sweep_kernel, out_shape=[jax.ShapeDtypeStruct(rows.shape,...  2.06 us
  transfers between devices with their start and end apart: 1, of which 1 were waited for; matrix products, arithmetic and copies ran while one was open for 0% of the time, Pallas kernels for 0%

profile of v4, /device:TPU:8, one launch (start us, length us, event | category | flops | bytes accessed | tf_op | source)
XLA Modules:
  0.0 100.4 jit_solution(11314029622161508629)
XLA Ops:
  0.6 0.0 copy-start
  0.7 1.3 %copy-done = f32[1,3,448,256]{3,2,1,0:T(8,128)S(1)} copy-done((f32[1,3,448,256]{3,2,1,0:T(8,128)S(1)}, f32[1,3,448,256]{3,2,1,0:T(8,128)}, u32[]{:S(2)}) %copy-start) | copy-done | bytes 1376280
  2.0 1.9 %collective-permute-start = (bf16[3,4,56,256]{3,2,1,0:T(8,128)(2,1)S(1)}, bf16[3,4,56,256]{3,2,1,0:T(8,128)(2,1)S(1)}, u32[]{:S(2)}, u32[]{:S(2)}) collective-permute-start(bf16[3,4,56,256]{3,2,1,0:T(8,128)(2,1)S(1)} %fusion.2), channel_id=1, source_target_pairs={{0,128},{128,0},{256,384},{384,256},{512,640},{640,512},{768,896},... | collective-permute-start | bytes 1032200 | tf_op jit(solution)/shard_map/ppermute | solution.py:182
  4.0 0.0 copy-start.1
  4.0 1.5 %collective-permute-done = bf16[3,4,56,256]{3,2,1,0:T(8,128)(2,1)S(1)} collective-permute-done((bf16[3,4,56,256]{3,2,1,0:T(8,128)(2,1)S(1)}, bf16[3,4,56,256]{3,2,1,0:T(8,128)(2,1)S(1)}, u32[]{:S(2)}, u32[]{:S(2)}) %collective-permute-start) | collective-permute-done | bytes 344096 | tf_op jit(solution)/shard_map/ppermute | solution.py:182
  5.6 0.1 fusion.1
  5.7 11.9 %all_to_all.20 = bf16[4,3,56,256]{3,2,1,0:T(8,128)(2,1)S(1)} all-to-all(bf16[4,3,56,256]{3,2,1,0:T(8,128)(2,1)S(1)} %copy.24), channel_id=1, replica_groups={{0,256,512,768},{128,384,640,896},{1,257,513,769},{129,385,641,897},{2,..., dimensions={0} | all-to-all | bytes 688128 | tf_op jit(solution)/shard_map/all_to_all | solution.py:187
  17.7 0.0 copy-done.1
  17.8 0.1 copy.27
  17.9 42.3 %all_to_all.21 = bf16[16,11,2,128]{3,2,1,0:T(2,128)(2,1)S(1)} all-to-all(bf16[16,11,2,128]{3,2,1,0:T(2,128)(2,1)S(1)} %copy.27), channel_id=1, replica_groups={{64,104,16,56,96,8,48,88,0,40,80,120,32,72,112,24},{65,105,17,57,97,9,4..., dimensions={0} | all-to-all | bytes 180224 | tf_op jit(solution)/shard_map/all_to_all | solution.py:198
  60.2 0.3 shard_map.41
  60.5 10.0 %all_to_all.22.grams_ref = f32[8,24,128]{2,1,0:T(8,128)S(1)} all-to-all(f32[8,24,128]{2,1,0:T(8,128)S(1)} %shard_map.41), channel_id=1, replica_groups={{2,3,0,1,6,7,4,5},{10,11,8,9,14,15,12,13},{18,19,16,17,22,23,20,21},{26..., dimensions={0} | all-to-all | bytes 196608 | tf_op jit(solution)/shard_map/all_to_all | solution.py:202
  70.5 2.1 %shard_map.42 = (bf16[352,128]{1,0:T(8,128)(2,1)S(1)}, f32[3,56,256]{2,1,0:T(8,128)}) custom-call(f32[8,24,128]{2,1,0:T(8,128)S(1)} %all_to_all.22.grams_ref, bf16[352,128]{1,0:T(8,128)(2,1)S(1)} %bitcast.41, f32[3,56,256]{2,1,0:T(8,128)S(1)} %get-tuple-element.8.momentum_ref), custom_call_target="tpu_custom_call" | custom-call | tf_op jit(solution)/shard_map/pallas_call | solution.py:203
  72.5 27.1 %all_to_all.23 = bf16[16,11,2,128]{3,2,1,0:T(2,128)(2,1)S(1)} all-to-all(bf16[16,11,2,128]{3,2,1,0:T(2,128)(2,1)S(1)} %bitcast.42), channel_id=1, replica_groups={{64,104,16,56,96,8,48,88,0,40,80,120,32,72,112,24},{65,105,17,57,97,9,4..., dimensions={0} | all-to-all | bytes 180224 | tf_op jit(solution)/shard_map/all_to_all | solution.py:215
  99.7 0.6 pad_maximum_fusion.1
  (19 shorter events, 0.3 us)
Async XLA Ops:
  0.6 1.3 %copy-start = (f32[1,3,448,256]{3,2,1,0:T(8,128)S(1)}, f32[1,3,448,256]{3,2,1,0:T(8,128)}, u32[]{:S(2)}) copy-start(f32[1,3,448,256]{3,2,1,0:T(8,128)} %param.2) | copy-start | bytes 4128772
  2.0 3.5 %collective-permute-start = (bf16[3,4,56,256]{3,2,1,0:T(8,128)(2,1)S(1)}, bf16[3,4,56,256]{3,2,1,0:T(8,128)(2,1)S(1)}, u32[]{:S(2)}, u32[]{:S(2)}) collective-permute-start(bf16[3,4,56,256]{3,2,1,0:T(8,128)(2,1)S(1)} %fusion.2), channel_id=1, source_target_pairs={{0,128},{128,0},{256,384},{384,256},{512,640},{640,512},{768,896},... | collective-permute-start | bytes 1032200 | tf_op jit(solution)/shard_map/ppermute | solution.py:182
  4.0 13.7 %copy-start.1 = (f32[3,56,256]{2,1,0:T(8,128)S(1)}, f32[3,56,256]{2,1,0:T(8,128)}, u32[]{:S(2)}) copy-start(f32[3,56,256]{2,1,0:T(8,128)} %param.3) | copy-start | bytes 516100

commit v5 on v4

--- a/solution.py
+++ b/solution.py
@@ -182,8 +182,10 @@
     arrived = lax.ppermute(sent, "dp", [(i, i ^ 1) for i in range(groups)])
     _, again = lax.optimization_barrier((sent, parts))
     own = lax.optimization_barrier(lax.dynamic_index_in_dim(again, core, 2, keepdims=False).astype(BF16))
-    pair = (own.astype(F32) + arrived.astype(F32)).astype(BF16).swapaxes(0, 1)
-    chips = [[chip * CORES + side for chip in range(groups // CORES)] for side in range(CORES)]
+    pair = (own.astype(F32) + arrived.astype(F32)).astype(BF16)
+    order = (2, 1, 0, 3)
+    pair = jnp.stack([pair[:, chip] for chip in order])
+    chips = [[chip * CORES + side for chip in order] for side in range(CORES)]
     arrived = lax.all_to_all(pair, "dp", 0, 0, tiled=True, axis_index_groups=chips)
     return jnp.sum(arrived.astype(F32), axis=0)
 

time: 101 us -> 99.9 us (0.989)
    all_to_all x1, blocking collectives: 11.9 us -> 10.6 us  [gather_sum(): lax.all_to_all(pair, 'dp', 0, 0, tiled=True, axis_index_groups=chips)]
where the time goes in v5:
time: 99.9 us; the launch traced here: 99.5 us
  blocking collectives  90.4 us (90%)
  Pallas kernels  2.31 us (2%)
  starting transfers between devices  1.92 us (2%)
  local copies, waits for them, and re-layouts  1.63 us (2%)
  waiting for transfers between devices  1.56 us (2%)
    all_to_all x1, blocking collectives, shards(): lax.all_to_all(outgoing, 'shard', 0, 0, tiled=True, axis_index_groups=own...  42.7 us
    all_to_all x1, blocking collectives, shards(): lax.all_to_all(finished, 'shard', 0, 0, tiled=True, axis_index_groups=own...  27.1 us
    all_to_all x1, blocking collectives, gather_sum(): lax.all_to_all(pair, 'dp', 0, 0, tiled=True, axis_index_groups=chips)  10.6 us
    all_to_all x1, blocking collectives, shards(): lax.all_to_all(parts, 'shard', 0, 0, tiled=True, axis_index_groups=chunk_...  10 us
    pallas_call x1, Pallas kernels, shards(): pl.pallas_call(sweep_kernel, out_shape=[jax.ShapeDtypeStruct(rows.shape,...  2.06 us
  transfers between devices with their start and end apart: 1, of which 1 were waited for; matrix products, arithmetic and copies ran while one was open for 0% of the time, Pallas kernels for 0%

profile of v5, /device:TPU:8, one launch (start us, length us, event | category | flops | bytes accessed | tf_op | source)
XLA Modules:
  0.0 99.5 jit_solution(10646132632720845678)
XLA Ops:
  0.6 0.0 copy-start
  0.7 1.3 %copy-done = f32[1,3,448,256]{3,2,1,0:T(8,128)S(1)} copy-done((f32[1,3,448,256]{3,2,1,0:T(8,128)S(1)}, f32[1,3,448,256]{3,2,1,0:T(8,128)}, u32[]{:S(2)}) %copy-start) | copy-done | bytes 1376280
  2.0 1.9 %collective-permute-start = (bf16[3,4,56,256]{3,2,1,0:T(8,128)(2,1)S(1)}, bf16[3,4,56,256]{3,2,1,0:T(8,128)(2,1)S(1)}, u32[]{:S(2)}, u32[]{:S(2)}) collective-permute-start(bf16[3,4,56,256]{3,2,1,0:T(8,128)(2,1)S(1)} %fusion.1), channel_id=1, source_target_pairs={{0,128},{128,0},{256,384},{384,256},{512,640},{640,512},{768,896},... | collective-permute-start | bytes 1032200 | tf_op jit(solution)/shard_map/ppermute | solution.py:182
  4.0 1.6 %collective-permute-done = bf16[3,4,56,256]{3,2,1,0:T(8,128)(2,1)S(1)} collective-permute-done((bf16[3,4,56,256]{3,2,1,0:T(8,128)(2,1)S(1)}, bf16[3,4,56,256]{3,2,1,0:T(8,128)(2,1)S(1)}, u32[]{:S(2)}, u32[]{:S(2)}) %collective-permute-start) | collective-permute-done | bytes 344096 | tf_op jit(solution)/shard_map/ppermute | solution.py:182
  5.6 0.1 add_convert_fusion
  5.7 0.0 copy-start.1
  5.8 10.6 %all_to_all.20 = bf16[4,3,56,256]{3,2,1,0:T(8,128)(2,1)S(1)} all-to-all(bf16[4,3,56,256]{3,2,1,0:T(8,128)(2,1)S(1)} %pad_maximum_fusion), channel_id=1, replica_groups={{512,256,0,768},{640,384,128,896},{513,257,1,769},{641,385,129,897},{51..., dimensions={0} | all-to-all | bytes 688128 | tf_op jit(solution)/shard_map/all_to_all | solution.py:189
  16.4 0.0 copy-done.1
  16.5 0.1 copy.32
  16.6 42.7 %all_to_all.21 = bf16[16,11,2,128]{3,2,1,0:T(2,128)(2,1)S(1)} all-to-all(bf16[16,11,2,128]{3,2,1,0:T(2,128)(2,1)S(1)} %copy.32), channel_id=1, replica_groups={{64,104,16,56,96,8,48,88,0,40,80,120,32,72,112,24},{65,105,17,57,97,9,4..., dimensions={0} | all-to-all | bytes 180224 | tf_op jit(solution)/shard_map/all_to_all | solution.py:200
  59.3 0.3 shard_map.41
  59.5 10.0 %all_to_all.22.grams_ref = f32[8,24,128]{2,1,0:T(8,128)S(1)} all-to-all(f32[8,24,128]{2,1,0:T(8,128)S(1)} %shard_map.41), channel_id=1, replica_groups={{2,3,0,1,6,7,4,5},{10,11,8,9,14,15,12,13},{18,19,16,17,22,23,20,21},{26..., dimensions={0} | all-to-all | bytes 196608 | tf_op jit(solution)/shard_map/all_to_all | solution.py:204
  69.6 2.1 %shard_map.42 = (bf16[352,128]{1,0:T(8,128)(2,1)S(1)}, f32[3,56,256]{2,1,0:T(8,128)}) custom-call(f32[8,24,128]{2,1,0:T(8,128)S(1)} %all_to_all.22.grams_ref, bf16[352,128]{1,0:T(8,128)(2,1)S(1)} %bitcast.53, f32[3,56,256]{2,1,0:T(8,128)S(1)} %get-tuple-element.8.momentum_ref), custom_call_target="tpu_custom_call" | custom-call | tf_op jit(solution)/shard_map/pallas_call | solution.py:205
  71.6 27.1 %all_to_all.23 = bf16[16,11,2,128]{3,2,1,0:T(2,128)(2,1)S(1)} all-to-all(bf16[16,11,2,128]{3,2,1,0:T(2,128)(2,1)S(1)} %bitcast.54), channel_id=1, replica_groups={{64,104,16,56,96,8,48,88,0,40,80,120,32,72,112,24},{65,105,17,57,97,9,4..., dimensions={0} | all-to-all | bytes 180224 | tf_op jit(solution)/shard_map/all_to_all | solution.py:217
  98.9 0.6 pad_maximum_fusion.2
  (20 shorter events, 0.4 us)
Async XLA Ops:
  0.6 1.3 %copy-start = (f32[1,3,448,256]{3,2,1,0:T(8,128)S(1)}, f32[1,3,448,256]{3,2,1,0:T(8,128)}, u32[]{:S(2)}) copy-start(f32[1,3,448,256]{3,2,1,0:T(8,128)} %param.2) | copy-start | bytes 4128772
  2.0 3.5 %collective-permute-start = (bf16[3,4,56,256]{3,2,1,0:T(8,128)(2,1)S(1)}, bf16[3,4,56,256]{3,2,1,0:T(8,128)(2,1)S(1)}, u32[]{:S(2)}, u32[]{:S(2)}) collective-permute-start(bf16[3,4,56,256]{3,2,1,0:T(8,128)(2,1)S(1)} %fusion.1), channel_id=1, source_target_pairs={{0,128},{128,0},{256,384},{384,256},{512,640},{640,512},{768,896},... | collective-permute-start | bytes 1032200 | tf_op jit(solution)/shard_map/ppermute | solution.py:182
  5.7 10.7 %copy-start.1 = (f32[3,56,256]{2,1,0:T(8,128)S(1)}, f32[3,56,256]{2,1,0:T(8,128)}, u32[]{:S(2)}) copy-start(f32[3,56,256]{2,1,0:T(8,128)} %param.3) | copy-start | bytes 516100

commit v6 on v5

--- a/solution.py
+++ b/solution.py
@@ -180,7 +180,8 @@
     parts = gradients.reshape(mats, groups // CORES, CORES, blocks // groups, width)
     sent = lax.dynamic_index_in_dim(parts, 1 - core, 2, keepdims=False).astype(BF16)
     arrived = lax.ppermute(sent, "dp", [(i, i ^ 1) for i in range(groups)])
-    _, again = lax.optimization_barrier((sent, parts))
+    _, again = lax.optimization_barrier((sent, gradients))
+    again = again.reshape(parts.shape)
     own = lax.optimization_barrier(lax.dynamic_index_in_dim(again, core, 2, keepdims=False).astype(BF16))
     pair = (own.astype(F32) + arrived.astype(F32)).astype(BF16)
     order = (2, 1, 0, 3)

time: 99.9 us -> 99.7 us (level)
  waiting for transfers between devices: 1.56 us -> 0.46 us
    unnamed x5 -> x3, local copies, waits for them, and re-layouts: 1.33 us -> 0.01 us
    convert_element_type x1, local copies, waits for them, and re-layouts: 0.04 us -> 1.14 us  [gather_sum(): lax.dynamic_index_in_dim(parts, 1 - core, 2, keepdims=False).astype(BF16)]
    convert_element_type x1, local copies, waits for them, and re-layouts: 0.04 us -> 1.14 us  [gather_sum(): lax.dynamic_index_in_dim(again, core, 2, keepdims=False).astype(BF16)]
    ppermute x1, waiting for transfers between devices: 1.56 us -> 0.46 us  [gather_sum(): arrived = lax.ppermute(sent, 'dp', [(i, i ^ 1) for i in range(groups)])]
  transfers between devices with their start and end apart: 1 -> 1, of which waited for: 1 -> 1; matrix products, arithmetic and copies ran while one was open for 0% -> 1% of each run, Pallas kernels for 0% -> 0%
where the time goes in v6:
time: 99.7 us; the launch traced here: 99.3 us
  blocking collectives  90.4 us (91%)
  local copies, waits for them, and re-layouts  2.52 us (3%)
  Pallas kernels  2.32 us (2%)
  starting transfers between devices  1.92 us (2%)
    all_to_all x1, blocking collectives, shards(): lax.all_to_all(outgoing, 'shard', 0, 0, tiled=True, axis_index_groups=own...  42.7 us
    all_to_all x1, blocking collectives, shards(): lax.all_to_all(finished, 'shard', 0, 0, tiled=True, axis_index_groups=own...  27.1 us
    all_to_all x1, blocking collectives, gather_sum(): lax.all_to_all(pair, 'dp', 0, 0, tiled=True, axis_index_groups=chips)  10.6 us
    all_to_all x1, blocking collectives, shards(): lax.all_to_all(parts, 'shard', 0, 0, tiled=True, axis_index_groups=chunk_...  10 us
    pallas_call x1, Pallas kernels, shards(): pl.pallas_call(sweep_kernel, out_shape=[jax.ShapeDtypeStruct(rows.shape,...  2.06 us
  transfers between devices with their start and end apart: 1, of which 1 were waited for; matrix products, arithmetic and copies ran while one was open for 1% of the time, Pallas kernels for 0%

profile of v6, /device:TPU:8, one launch (start us, length us, event | category | flops | bytes accessed | tf_op | source)
XLA Modules:
  0.0 99.3 jit_solution(11341902353463957754)
XLA Ops:
  0.6 1.1 %fusion.1 = bf16[3,4,56,256]{3,2,1,0:T(8,128)(2,1)S(1)} fusion(f32[3,4,2,56,256]{4,3,2,1,0:T(8,128)} %bitcast.60, s32[]{:T(128)S(6)} %select_n.15), kind=kLoop, calls=%fused_computation.5 | loop fusion | bytes 688132 | tf_op jit(solution)/shard_map/convert_element_type | solution.py:181
  1.8 1.9 %collective-permute-start = (bf16[3,4,56,256]{3,2,1,0:T(8,128)(2,1)S(1)}, bf16[3,4,56,256]{3,2,1,0:T(8,128)(2,1)S(1)}, u32[]{:S(2)}, u32[]{:S(2)}) collective-permute-start(bf16[3,4,56,256]{3,2,1,0:T(8,128)(2,1)S(1)} %fusion.1), channel_id=1, source_target_pairs={{0,128},{128,0},{256,384},{384,256},{512,640},{640,512},{768,896},... | collective-permute-start | bytes 1032200 | tf_op jit(solution)/shard_map/ppermute | solution.py:182
  3.7 1.1 %fusion = bf16[3,4,56,256]{3,2,1,0:T(8,128)(2,1)S(1)} fusion(f32[3,4,2,56,256]{4,3,2,1,0:T(8,128)} %bitcast.61, s32[]{:T(128)S(6)} %select_n.16), kind=kLoop, calls=%fused_computation.4 | loop fusion | bytes 688132 | tf_op jit(solution)/shard_map/convert_element_type | solution.py:185
  4.9 0.5 collective-permute-done
  5.3 0.1 add_convert_fusion
  5.4 0.0 copy-start
  5.5 10.6 %all_to_all.20 = bf16[4,3,56,256]{3,2,1,0:T(8,128)(2,1)S(1)} all-to-all(bf16[4,3,56,256]{3,2,1,0:T(8,128)(2,1)S(1)} %pad_maximum_fusion), channel_id=1, replica_groups={{512,256,0,768},{640,384,128,896},{513,257,1,769},{641,385,129,897},{51..., dimensions={0} | all-to-all | bytes 688128 | tf_op jit(solution)/shard_map/all_to_all | solution.py:190
  16.1 0.0 copy-done
  16.3 0.1 copy.32
  16.4 42.7 %all_to_all.21 = bf16[16,11,2,128]{3,2,1,0:T(2,128)(2,1)S(1)} all-to-all(bf16[16,11,2,128]{3,2,1,0:T(2,128)(2,1)S(1)} %copy.32), channel_id=1, replica_groups={{64,104,16,56,96,8,48,88,0,40,80,120,32,72,112,24},{65,105,17,57,97,9,4..., dimensions={0} | all-to-all | bytes 180224 | tf_op jit(solution)/shard_map/all_to_all | solution.py:201
  59.1 0.3 shard_map.41
  59.3 10.0 %all_to_all.22.grams_ref = f32[8,24,128]{2,1,0:T(8,128)S(1)} all-to-all(f32[8,24,128]{2,1,0:T(8,128)S(1)} %shard_map.41), channel_id=1, replica_groups={{2,3,0,1,6,7,4,5},{10,11,8,9,14,15,12,13},{18,19,16,17,22,23,20,21},{26..., dimensions={0} | all-to-all | bytes 196608 | tf_op jit(solution)/shard_map/all_to_all | solution.py:205
  69.4 2.1 %shard_map.42 = (bf16[352,128]{1,0:T(8,128)(2,1)S(1)}, f32[3,56,256]{2,1,0:T(8,128)}) custom-call(f32[8,24,128]{2,1,0:T(8,128)S(1)} %all_to_all.22.grams_ref, bf16[352,128]{1,0:T(8,128)(2,1)S(1)} %bitcast.53, f32[3,56,256]{2,1,0:T(8,128)S(1)} %get-tuple-element.8.momentum_ref), custom_call_target="tpu_custom_call" | custom-call | tf_op jit(solution)/shard_map/pallas_call | solution.py:206
  71.4 27.1 %all_to_all.23 = bf16[16,11,2,128]{3,2,1,0:T(2,128)(2,1)S(1)} all-to-all(bf16[16,11,2,128]{3,2,1,0:T(2,128)(2,1)S(1)} %bitcast.54), channel_id=1, replica_groups={{64,104,16,56,96,8,48,88,0,40,80,120,32,72,112,24},{65,105,17,57,97,9,4..., dimensions={0} | all-to-all | bytes 180224 | tf_op jit(solution)/shard_map/all_to_all | solution.py:218
  98.7 0.6 pad_maximum_fusion.2
  (18 shorter events, 0.3 us)
Async XLA Ops:
  1.8 3.5 %collective-permute-start = (bf16[3,4,56,256]{3,2,1,0:T(8,128)(2,1)S(1)}, bf16[3,4,56,256]{3,2,1,0:T(8,128)(2,1)S(1)}, u32[]{:S(2)}, u32[]{:S(2)}) collective-permute-start(bf16[3,4,56,256]{3,2,1,0:T(8,128)(2,1)S(1)} %fusion.1), channel_id=1, source_target_pairs={{0,128},{128,0},{256,384},{384,256},{512,640},{640,512},{768,896},... | collective-permute-start | bytes 1032200 | tf_op jit(solution)/shard_map/ppermute | solution.py:182
  5.4 10.7 %copy-start = (f32[3,56,256]{2,1,0:T(8,128)S(1)}, f32[3,56,256]{2,1,0:T(8,128)}, u32[]{:S(2)}) copy-start(f32[3,56,256]{2,1,0:T(8,128)} %param.3) | copy-start | bytes 516100

commit v7 on v6

--- a/solution.py
+++ b/solution.py
@@ -165,7 +165,7 @@
 
 def owner_groups():
     chunks = C // 256
-    return [[(row * 5 + 8) % BR * chunks + chunk for row in range(BR)] for chunk in range(chunks)]
+    return [[(row * 5 + 9) % BR * chunks + chunk for row in range(BR)] for chunk in range(chunks)]
 
 
 def chunk_groups():

time: 99.7 us -> 100 us (level)
  no operation moved by 1% of the time
where the time goes in v7:
time: 100 us; the launch traced here: 99.6 us
  blocking collectives  90.7 us (91%)
  local copies, waits for them, and re-layouts  2.52 us (3%)
  Pallas kernels  2.31 us (2%)
  starting transfers between devices  1.92 us (2%)
    all_to_all x1, blocking collectives, shards(): lax.all_to_all(outgoing, 'shard', 0, 0, tiled=True, axis_index_groups=own...  43 us
    all_to_all x1, blocking collectives, shards(): lax.all_to_all(finished, 'shard', 0, 0, tiled=True, axis_index_groups=own...  28.1 us
    all_to_all x1, blocking collectives, gather_sum(): lax.all_to_all(pair, 'dp', 0, 0, tiled=True, axis_index_groups=chips)  10.6 us
    all_to_all x1, blocking collectives, shards(): lax.all_to_all(parts, 'shard', 0, 0, tiled=True, axis_index_groups=chunk_...  9.06 us
    pallas_call x1, Pallas kernels, shards(): pl.pallas_call(sweep_kernel, out_shape=[jax.ShapeDtypeStruct(rows.shape,...  2.06 us
  transfers between devices with their start and end apart: 1, of which 1 were waited for; matrix products, arithmetic and copies ran while one was open for 1% of the time, Pallas kernels for 0%

profile of v7, /device:TPU:8, one launch (start us, length us, event | category | flops | bytes accessed | tf_op | source)
XLA Modules:
  0.0 99.6 jit_solution(139244451662418659)
XLA Ops:
  0.6 1.1 %fusion.1 = bf16[3,4,56,256]{3,2,1,0:T(8,128)(2,1)S(1)} fusion(f32[3,4,2,56,256]{4,3,2,1,0:T(8,128)} %bitcast.60, s32[]{:T(128)S(6)} %select_n.15), kind=kLoop, calls=%fused_computation.5 | loop fusion | bytes 688132 | tf_op jit(solution)/shard_map/convert_element_type | solution.py:181
  1.8 1.9 %collective-permute-start = (bf16[3,4,56,256]{3,2,1,0:T(8,128)(2,1)S(1)}, bf16[3,4,56,256]{3,2,1,0:T(8,128)(2,1)S(1)}, u32[]{:S(2)}, u32[]{:S(2)}) collective-permute-start(bf16[3,4,56,256]{3,2,1,0:T(8,128)(2,1)S(1)} %fusion.1), channel_id=1, source_target_pairs={{0,128},{128,0},{256,384},{384,256},{512,640},{640,512},{768,896},... | collective-permute-start | bytes 1032200 | tf_op jit(solution)/shard_map/ppermute | solution.py:182
  3.7 1.1 %fusion = bf16[3,4,56,256]{3,2,1,0:T(8,128)(2,1)S(1)} fusion(f32[3,4,2,56,256]{4,3,2,1,0:T(8,128)} %bitcast.61, s32[]{:T(128)S(6)} %select_n.16), kind=kLoop, calls=%fused_computation.4 | loop fusion | bytes 688132 | tf_op jit(solution)/shard_map/convert_element_type | solution.py:185
  4.9 0.5 collective-permute-done
  5.3 0.1 add_convert_fusion
  5.4 0.0 copy-start
  5.5 10.6 %all_to_all.20 = bf16[4,3,56,256]{3,2,1,0:T(8,128)(2,1)S(1)} all-to-all(bf16[4,3,56,256]{3,2,1,0:T(8,128)(2,1)S(1)} %pad_maximum_fusion), channel_id=1, replica_groups={{512,256,0,768},{640,384,128,896},{513,257,1,769},{641,385,129,897},{51..., dimensions={0} | all-to-all | bytes 688128 | tf_op jit(solution)/shard_map/all_to_all | solution.py:190
  16.1 0.0 copy-done
  16.3 0.1 copy.32
  16.4 43.0 %all_to_all.21 = bf16[16,11,2,128]{3,2,1,0:T(2,128)(2,1)S(1)} all-to-all(bf16[16,11,2,128]{3,2,1,0:T(2,128)(2,1)S(1)} %copy.32), channel_id=1, replica_groups={{72,112,24,64,104,16,56,96,8,48,88,0,40,80,120,32},{73,113,25,65,105,17..., dimensions={0} | all-to-all | bytes 180224 | tf_op jit(solution)/shard_map/all_to_all | solution.py:201
  59.4 0.3 shard_map.41
  59.6 9.1 %all_to_all.22.grams_ref = f32[8,24,128]{2,1,0:T(8,128)S(1)} all-to-all(f32[8,24,128]{2,1,0:T(8,128)S(1)} %shard_map.41), channel_id=1, replica_groups={{2,3,0,1,6,7,4,5},{10,11,8,9,14,15,12,13},{18,19,16,17,22,23,20,21},{26..., dimensions={0} | all-to-all | bytes 196608 | tf_op jit(solution)/shard_map/all_to_all | solution.py:205
  68.7 2.1 %shard_map.42 = (bf16[352,128]{1,0:T(8,128)(2,1)S(1)}, f32[3,56,256]{2,1,0:T(8,128)}) custom-call(f32[8,24,128]{2,1,0:T(8,128)S(1)} %all_to_all.22.grams_ref, bf16[352,128]{1,0:T(8,128)(2,1)S(1)} %bitcast.53, f32[3,56,256]{2,1,0:T(8,128)S(1)} %get-tuple-element.8.momentum_ref), custom_call_target="tpu_custom_call" | custom-call | tf_op jit(solution)/shard_map/pallas_call | solution.py:206
  70.8 28.1 %all_to_all.23 = bf16[16,11,2,128]{3,2,1,0:T(2,128)(2,1)S(1)} all-to-all(bf16[16,11,2,128]{3,2,1,0:T(2,128)(2,1)S(1)} %bitcast.54), channel_id=1, replica_groups={{72,112,24,64,104,16,56,96,8,48,88,0,40,80,120,32},{73,113,25,65,105,17..., dimensions={0} | all-to-all | bytes 180224 | tf_op jit(solution)/shard_map/all_to_all | solution.py:218
  99.0 0.6 pad_maximum_fusion.2
  (18 shorter events, 0.3 us)
Async XLA Ops:
  1.8 3.5 %collective-permute-start = (bf16[3,4,56,256]{3,2,1,0:T(8,128)(2,1)S(1)}, bf16[3,4,56,256]{3,2,1,0:T(8,128)(2,1)S(1)}, u32[]{:S(2)}, u32[]{:S(2)}) collective-permute-start(bf16[3,4,56,256]{3,2,1,0:T(8,128)(2,1)S(1)} %fusion.1), channel_id=1, source_target_pairs={{0,128},{128,0},{256,384},{384,256},{512,640},{640,512},{768,896},... | collective-permute-start | bytes 1032200 | tf_op jit(solution)/shard_map/ppermute | solution.py:182
  5.4 10.7 %copy-start = (f32[3,56,256]{2,1,0:T(8,128)S(1)}, f32[3,56,256]{2,1,0:T(8,128)}, u32[]{:S(2)}) copy-start(f32[3,56,256]{2,1,0:T(8,128)} %param.3) | copy-start | bytes 516100
